TPU v7x, 256 devices: a whole 4x4x8 slice. The times are simulated.
256 devices in a mesh: dom: 64 (over z, y, core), rep: 4 (over x).
Axes of the slice: x: 4, y: 4, z: 8, core: 2. Of those that a mesh axis runs over, the one named last changes fastest.
Arguments:
- features: bfloat16 [65536, 512], P('dom', 'rep'), may hold values from -6 to 6
- weight: bfloat16 [512, 512], P(None, 'rep'), may hold values from -0.25 to 0.25
- bias: bfloat16 [512], P('rep'), may hold values from -3 to 3
- cotangent: bfloat16 [65536, 512], P('dom', 'rep'), may hold values from -6 to 6
- tile_vals: bfloat16 [64, 160, 128, 128], P('dom'), may hold values from -0.21875 to 0.21875
- tile_row: int32 [64, 160], P('dom'), may hold values from 0 to 8, as said below
- tile_src: int32 [64, 160], P('dom'), may hold values from 0 to 135, as said below
- send_blocks: int32 [64, 64, 2], P('dom'), may hold values from 0 to 7
- send_count: int32 [64, 64], P('dom'), may hold values from 0 to 2, as said below
Outputs:
- out: bfloat16 [65536, 512], P('dom', 'rep')
- grad_input: bfloat16 [65536, 512], P('dom', 'rep')
- grad_weight: float32 [512, 512], P(None, 'rep')
- grad_bias: float32 [512], P('rep')
Inputs may be any that keep to these rules, and one draw needn't show every extreme that they name: Partition q sends the first send_count[q, p] entries of send_blocks[q, p] to partition p; send_count[q, q] = 0, and every partition sends 2 blocks to some partition. `tile_row`: 8 marks an unused slot. Slots below 32 take own blocks; slot 32 + q * 2 + c is used only if c < send_count[q, p]. Partition 0 uses all its own-block slots. `tile_src`: slots below 32 name an own block below 8; slot 32 + m names source slot 8 + m.
All inputs are finite; a program needn't handle non-finite values.
Results may differ from a plain program's by a relative error of at most 0.007.
Values may be sent and summed in bfloat16 or wider, within the bound.
A program may use at most 128 MiB of HBM per device.

v0:
```python
import jax
import jax.numpy as jnp
from jax import lax
from jax.sharding import PartitionSpec as P

B = 128
NB = 8
CAP = 2


def receive_blocks(outgoing, peer_count, panel_width):
    arrived = lax.all_to_all(outgoing, "dom", split_axis=0, concat_axis=0, tiled=True)
    return arrived.reshape(peer_count * CAP, B, panel_width)


def shards(
    features, weight, bias, cotangent, tile_vals, tile_row, tile_src, send_blocks, send_count
):
    row_count, panel_width = features.shape
    peer_count = lax.axis_size("dom")
    gathered = lax.all_gather(features, "rep", axis=1, tiled=True)
    hidden = jnp.dot(gathered, weight, preferred_element_type=jnp.float32).astype(jnp.bfloat16)
    hidden_blocks = hidden.reshape(NB, B, panel_width)
    targets = send_blocks[0]
    counts = send_count[0]
    keep_slot = jnp.arange(CAP, dtype=jnp.int32)[None, :] < counts[:, None]
    outgoing = hidden_blocks[targets]
    outgoing = jnp.where(keep_slot[:, :, None, None], outgoing, jnp.zeros_like(outgoing))
    tile_set = tile_vals[0]
    tile_rows = tile_row[0]
    tile_sources = tile_src[0]
    arrived = receive_blocks(outgoing, peer_count, panel_width)
    sources = jnp.concatenate([hidden_blocks, arrived], 0)
    product = jnp.einsum(
        "kab,kbf->kaf", tile_set, sources[tile_sources], preferred_element_type=jnp.float32
    )
    aggregate = jax.ops.segment_sum(product, tile_rows, NB + 1)[:NB]
    shifted = aggregate.reshape(row_count, panel_width) + bias.astype(jnp.float32)
    sigma = jax.nn.sigmoid(shifted)
    out = (shifted * sigma).astype(jnp.bfloat16)
    grad_pre = (cotangent.astype(jnp.float32) * sigma * (1.0 + shifted * (1.0 - sigma))).astype(
        jnp.bfloat16
    )
    pre_padded = jnp.concatenate(
        [grad_pre.reshape(NB, B, panel_width), jnp.zeros((1, B, panel_width), jnp.bfloat16)], 0
    )
    contrib = jnp.einsum(
        "kab,kaf->kbf", tile_set, pre_padded[tile_rows], preferred_element_type=jnp.float32
    )
    per_slot = jax.ops.segment_sum(contrib, tile_sources, NB + peer_count * CAP)
    outbound = per_slot[NB:].reshape(peer_count, CAP, B, panel_width)
    returned = lax.all_to_all(outbound, "dom", split_axis=0, concat_axis=0, tiled=True)
    own_blocks = per_slot[:NB]
    returned = jnp.where(keep_slot[:, :, None, None], returned, jnp.zeros_like(returned))
    grad_blocks = own_blocks + jax.ops.segment_sum(
        returned.reshape(peer_count * CAP, B, panel_width), targets.reshape(-1), NB
    )
    grad_agg = grad_blocks.reshape(row_count, panel_width).astype(jnp.bfloat16)
    weight_part = jnp.dot(gathered.T, grad_agg, preferred_element_type=jnp.float32)
    bias_part = jnp.sum(grad_pre.astype(jnp.float32), 0)
    grad_weight, grad_bias = lax.psum((weight_part, bias_part), "dom")
    partial_terms = jnp.dot(grad_agg, weight.T, preferred_element_type=jnp.float32)
    grad_input = lax.psum_scatter(partial_terms, "rep", scatter_dimension=1, tiled=True).astype(
        jnp.bfloat16
    )
    return (out, grad_input, grad_weight, grad_bias)


def solution(mesh):
    in_specs = (
        P("dom", "rep"),
        P(None, "rep"),
        P("rep"),
        P("dom", "rep"),
        P("dom", None, None, None),
        P("dom", None),
        P("dom", None),
        P("dom", None, None),
        P("dom", None),
    )
    out_specs = (P("dom", "rep"), P("dom", "rep"), P(None, "rep"), P("rep"))
    return jax.shard_map(shards, mesh=mesh, in_specs=in_specs, out_specs=out_specs, check_vma=False)
```

profile of v0, /device:TPU:1, one launch (start us, length us, event | category | flops | bytes accessed | tf_op | source)
XLA Modules:
  0.0 723.8 jit_solution(12466726873163206390)
XLA Ops:
  7.9 0.7 compare_select_fusion.2
  8.9 0.7 iota_compare_fusion
  9.6 31.6 %all-gather.2.cloned.1.call-done = bf16[1024,512]{1,0:T(8,128)(2,1)} async-done(((bf16[1024,128]{1,0:T(8,128)(2,1)}), bf16[1024,512]{1,0:T(8,128)(2,1)}) %all-gather.2.cloned.1.call-update) | async-done | bytes 1048592 | tf_op jit(solution)/shard_map/all_gather | solution.py:21
  41.2 1.7 convolution_convert_fusion
  42.8 3.0 gather_fusion
  45.9 4.5 broadcast_select_fusion.1
  50.4 11.9 %all-to-all-start = ((bf16[64,2,128,128]{3,2,1,0:T(8,128)(2,1)}), bf16[64,2,128,128]{3,2,1,0:T(8,128)(2,1)}, u32[]{:S(2)}, u32[]{:S(2)}) async-start(bf16[64,2,128,128]{3,2,1,0:T(8,128)(2,1)} %broadcast_select_fusion.1), calls=%async_computation | async-start | bytes 8388608 | tf_op jit(solution)/shard_map/all_to_all | solution.py:12
  62.4 94.3 %all-to-all-done = bf16[64,2,128,128]{3,2,1,0:T(8,128)(2,1)} async-done(((bf16[64,2,128,128]{3,2,1,0:T(8,128)(2,1)}), bf16[64,2,128,128]{3,2,1,0:T(8,128)(2,1)}, u32[]{:S(2)}, u32[]{:S(2)}) %all-to-all-start) | async-done | bytes 4194336 | tf_op jit(solution)/shard_map/all_to_all | solution.py:12
  156.7 4.6 pad_maximum_fusion
  161.3 10.0 %gather_fusion.1 = bf16[160,128,128]{2,1,0:T(8,128)(2,1)} fusion(bf16[136,128,128]{2,1,0:T(8,128)(2,1)} %pad_maximum_fusion, s32[1024]{0:T(1024)S(1)} %pad_clamp_fusion.1), kind=kCustom, calls=%fused_computation.1 | custom fusion | bytes 10486400 | tf_op jit(solution)/shard_map/gather | solution.py:35
  171.3 11.8 %fusion.4 = f32[160,128,128]{1,2,0:T(8,128)} fusion(bf16[160,128,128]{2,1,0:T(8,128)(2,1)} %gather_fusion.1, bf16[1,160,128,128]{3,2,1,0:T(8,128)(2,1)} %param.13), kind=kOutput, calls=%fused_computation.13 | convolution fusion | flops 671088640 | bytes 20971520 | tf_op jit(solution)/shard_map/kab,kbf->kaf/dot_general | solution.py:34
  183.2 11.7 %copy.20 = f32[160,128,128]{2,1,0:T(8,128)} copy(f32[160,128,128]{1,2,0:T(8,128)} %fusion.4) | data formatting | bytes 20971520 | tf_op jit(solution)/shard_map/kab,kbf->kaf/dot_general | solution.py:34
  194.9 21.1 %scatter_fusion = f32[9,128,128]{2,1,0:T(8,128)S(1)} fusion(f32[9,128,128]{2,1,0:T(8,128)S(1)} %broadcast_in_dim.19, s32[160]{0:T(256)S(1)} %bitcast.58, f32[160,128,128]{2,1,0:T(8,128)} %copy.20), kind=kCustom, calls=%fused_computation.3 | custom fusion | flops 2621440 | bytes 31457920 | tf_op jit(solution)/shard_map/scatter-add | solution.py:37
  216.2 1.0 convert_reduce_fusion
  217.2 7.5 %gather_fusion.2 = bf16[160,128,128]{2,1,0:T(8,128)(2,1)} fusion(bf16[9,128,128]{2,1,0:T(8,128)(2,1)S(1)} %concatenate.7, s32[1024]{0:T(1024)S(1)} %pad_clamp_fusion), kind=kCustom, calls=%fused_computation.2 | custom fusion | bytes 10486400 | tf_op jit(solution)/shard_map/gather | solution.py:48
  224.6 9.8 %fusion.7 = f32[160,128,128]{1,2,0:T(8,128)} fusion(bf16[160,128,128]{2,1,0:T(8,128)(2,1)} %gather_fusion.2, bf16[1,160,128,128]{3,2,1,0:T(8,128)(2,1)} %param.13), kind=kOutput, calls=%fused_computation.14 | convolution fusion | flops 671088640 | bytes 20971520 | tf_op jit(solution)/shard_map/kab,kaf->kbf/dot_general | solution.py:47
  234.4 11.8 %copy.22 = f32[160,128,128]{2,1,0:T(8,128)} copy(f32[160,128,128]{1,2,0:T(8,128)} %fusion.7) | data formatting | bytes 20971520 | tf_op jit(solution)/shard_map/kab,kaf->kbf/dot_general | solution.py:47
  246.2 4.6 broadcast_in_dim.38
  250.8 33.2 %scatter_fusion.1 = f32[136,128,128]{2,1,0:T(8,128)} fusion(f32[136,128,128]{2,1,0:T(8,128)} %broadcast_in_dim.38, s32[160]{0:T(256)S(1)} %bitcast.59, f32[160,128,128]{2,1,0:T(8,128)} %copy.22), kind=kCustom, calls=%fused_computation.4 | custom fusion | flops 2621440 | bytes 31457920 | tf_op jit(solution)/shard_map/scatter-add | solution.py:50
  284.0 7.9 %slice.20 = f32[128,128,128]{2,1,0:T(8,128)} slice(f32[136,128,128]{2,1,0:T(8,128)} %scatter_fusion.1), slice={[8:136], [0:128], [0:128]} | slice | bytes 16777216 | tf_op jit(solution)/shard_map/slice | solution.py:51
  291.8 7.6 %all-to-all-start.1 = ((f32[64,2,128,128]{3,2,1,0:T(8,128)}), f32[64,2,128,128]{3,2,1,0:T(8,128)}, u32[]{:S(2)}, u32[]{:S(2)}) async-start(f32[64,2,128,128]{3,2,1,0:T(8,128)} %bitcast.52), calls=%async_computation.1 | async-start | bytes 16777216 | tf_op jit(solution)/shard_map/all_to_all | solution.py:52
  299.7 1.1 slice.19
  300.8 181.5 %all-to-all-done.1 = f32[64,2,128,128]{3,2,1,0:T(8,128)} async-done(((f32[64,2,128,128]{3,2,1,0:T(8,128)}), f32[64,2,128,128]{3,2,1,0:T(8,128)}, u32[]{:S(2)}, u32[]{:S(2)}) %all-to-all-start.1) | async-done | bytes 8388640 | tf_op jit(solution)/shard_map/all_to_all | solution.py:52
  482.3 7.2 broadcast_select_fusion
  489.6 17.0 %scatter_fusion.2 = f32[8,128,128]{2,1,0:T(8,128)S(1)} fusion(f32[8,128,128]{2,1,0:T(8,128)S(1)} %slice.19, s32[128]{0:T(128)S(1)} %reshape.185, f32[128,128,128]{2,1,0:T(8,128)} %bitcast.53), kind=kCustom, calls=%fused_computation.5 | custom fusion | flops 2097152 | bytes 25166336 | tf_op jit(solution)/shard_map/scatter-add | solution.py:55
  506.6 1.0 convolution_bitcast_fusion
  507.7 1.8 fusion.10
  509.6 127.7 %psum.15 = f32[128]{0:T(128)} all-reduce(f32[128]{0:T(128)S(1)} %get-tuple-element.12), channel_id=1, replica_groups=mesh['dom'=64,'rep'=4] {'dom'}, use_global_device_ids=true, to_apply=%region_6.7 | all-reduce | flops 128 | bytes 1024 | tf_op jit(solution)/shard_map/psum | solution.py:61
  637.3 46.1 %all-reduce.3.cloned.1.call-done = f32[512,128]{0,1:T(8,128)} async-done(((f32[512,128]{0,1:T(8,128)}), f32[512,128]{0,1:T(8,128)}) %all-reduce.3.cloned.1.call-update) | async-done | bytes 262160 | tf_op jit(solution)/shard_map/psum | solution.py:61
  683.4 1.8 copy.24
  685.1 30.4 %reduce-scatter.2.cloned.1.call-done = f32[1024,128]{1,0:T(8,128)} async-done(((f32[1024,512]{1,0:T(8,128)}), f32[1024,128]{1,0:T(8,128)}) %reduce-scatter.2.cloned.1.call-update) | async-done | bytes 524304 | tf_op jit(solution)/shard_map/reduce_scatter | solution.py:63
  715.5 1.8 convert_element_type.34
  (34 shorter events, 1.5 us)
Async XLA Ops:
  7.2 34.0 %copy-start = (bf16[512,128]{1,0:T(8,128)(2,1)S(1)}, bf16[512,128]{1,0:T(8,128)(2,1)}, u32[]{:S(2)}) copy-start(bf16[512,128]{1,0:T(8,128)(2,1)} %param.10) | copy-start | bytes 393220
  7.2 34.0 %all-gather.2.cloned.1.call-start = ((), (), s32[]{:S(2)}) async-start(), calls=%async_computation.3 | async-start | bytes 1310720 | tf_op jit(solution)/shard_map/all_gather | solution.py:21
  50.4 11.9 %copy-start.6 = (bf16[128]{0:T(256)(128)(2,1)S(1)}, bf16[128]{0:T(256)(128)(2,1)}, u32[]{:S(2)}) copy-start(bf16[128]{0:T(256)(128)(2,1)} %param.11) | copy-start | bytes 772
  50.4 11.9 %copy-start.4 = (s32[1,160]{1,0:T(1,128)S(1)}, s32[1,160]{1,0:T(1,128)}, u32[]{:S(2)}) copy-start(s32[1,160]{1,0:T(1,128)} %param.15) | copy-start | bytes 1924
  50.4 12.0 %copy-start.3 = (s32[1,160]{1,0:T(1,128)S(1)}, s32[1,160]{1,0:T(1,128)}, u32[]{:S(2)}) copy-start(s32[1,160]{1,0:T(1,128)} %param.14) | copy-start | bytes 1924
  50.4 106.3 %all-to-all-start = ((bf16[64,2,128,128]{3,2,1,0:T(8,128)(2,1)}), bf16[64,2,128,128]{3,2,1,0:T(8,128)(2,1)}, u32[]{:S(2)}, u32[]{:S(2)}) async-start(bf16[64,2,128,128]{3,2,1,0:T(8,128)(2,1)} %broadcast_select_fusion.1), calls=%async_computation | async-start | bytes 8388608 | tf_op jit(solution)/shard_map/all_to_all | solution.py:12
  194.9 21.2 %copy-start.2 = (bf16[1024,128]{1,0:T(8,128)(2,1)S(1)}, bf16[1024,128]{1,0:T(8,128)(2,1)}, u32[]{:S(2)}) copy-start(bf16[1024,128]{1,0:T(8,128)(2,1)} %param.12) | copy-start | bytes 786436
  291.8 7.7 %copy-start.5 = (s32[1,64,2]{1,2,0:T(2,128)S(1)}, s32[1,64,2]{1,2,0:T(2,128)}, u32[]{:S(2)}) copy-start(s32[1,64,2]{1,2,0:T(2,128)} %param.16) | copy-start | bytes 1540
  291.8 190.5 %all-to-all-start.1 = ((f32[64,2,128,128]{3,2,1,0:T(8,128)}), f32[64,2,128,128]{3,2,1,0:T(8,128)}, u32[]{:S(2)}, u32[]{:S(2)}) async-start(f32[64,2,128,128]{3,2,1,0:T(8,128)} %bitcast.52), calls=%async_computation.1 | async-start | bytes 16777216 | tf_op jit(solution)/shard_map/all_to_all | solution.py:52
  299.4 383.9 %all-reduce.3.cloned.1.call-start = ((), (), s32[]{:S(2)}) async-start(), calls=%async_computation.5 | async-start | bytes 524288 | tf_op jit(solution)/shard_map/psum | solution.py:61
  489.5 17.1 %copy-start.1 = (bf16[1024,512]{1,0:T(8,128)(2,1)S(1)}, bf16[1024,512]{1,0:T(8,128)(2,1)}, u32[]{:S(2)}) copy-start(bf16[1024,512]{1,0:T(8,128)(2,1)} %all-gather.2.cloned.1.call-done) | copy-start | bytes 3145732
  507.7 207.8 %reduce-scatter.2.cloned.1.call-start = ((), (), s32[]{:S(2)}) async-start(), calls=%async_computation.4 | async-start | bytes 2621440 | tf_op jit(solution)/shard_map/reduce_scatter | solution.py:63
Sparse Core Ops, SparseCore 0:
  9.8 31.3 all-gather.1
  507.8 175.4 all-reduce.2
  686.1 29.4 reduce-scatter.1
where the time goes:
time: 726 us; the launch traced here: 724 us
  waiting for transfers between devices  385 us (53%)
  blocking collectives  128 us (18%)
  other arithmetic  91.9 us (13%)
  local copies, waits for them, and re-layouts  60 us (8%)
  matrix products  26.1 us (4%)
  starting transfers between devices  19.6 us (3%)
  between operations  13.9 us (2%)
    all_to_all x1, waiting for transfers between devices, shards(): lax.all_to_all(outbound, 'dom', split_axis=0, concat_axis=0, tiled=True)  182 us
    psum x1, blocking collectives, shards(): grad_weight, grad_bias = lax.psum((weight_part, bias_part), 'dom')  128 us
    all_to_all x1, waiting for transfers between devices, receive_blocks(): lax.all_to_all(outgoing, 'dom', split_axis=0, concat_axis=0, tiled=True)  94.3 us
    psum x1, waiting for transfers between devices, shards(): grad_weight, grad_bias = lax.psum((weight_part, bias_part), 'dom')  46.1 us
    scatter-add x1, other arithmetic, shards(): per_slot = jax.ops.segment_sum(contrib, tile_sources, NB + peer_count * CAP)  33.2 us
    all_gather x1, waiting for transfers between devices, shards(): gathered = lax.all_gather(features, 'rep', axis=1, tiled=True)  31.6 us
    reduce_scatter x1, waiting for transfers between devices, shards(): lax.psum_scatter(partial_terms, 'rep', scatter_dimension=1, tiled=True)  30.4 us
    scatter-add x1, other arithmetic, shards(): aggregate = jax.ops.segment_sum(product, tile_rows, NB + 1)[:NB]  21.1 us
  transfers between devices with their start and end apart: 5, of which 5 were waited for; matrix products, arithmetic and copies ran while one was open for 1% of the time, Pallas kernels for 0%

commit v1 on v0

--- a/solution.py
+++ b/solution.py
@@ -18,7 +18,12 @@
 ):
     row_count, panel_width = features.shape
     peer_count = lax.axis_size("dom")
-    gathered = lax.all_gather(features, "rep", axis=1, tiled=True)
+    ring = [features]
+    for hop in range(3):
+        ring.append(lax.ppermute(ring[-1], "rep", [(dev, (dev + 1) % 4) for dev in range(4)]))
+    gathered = jnp.roll(
+        jnp.concatenate(ring[::-1], axis=1), (lax.axis_index("rep") + 1) * ring[0].shape[1], axis=1
+    )
     hidden = jnp.dot(gathered, weight, preferred_element_type=jnp.float32).astype(jnp.bfloat16)
     hidden_blocks = hidden.reshape(NB, B, panel_width)
     targets = send_blocks[0]

time: 726 us -> 693 us (0.955)
  waiting for transfers between devices: 385 us -> 337 us
  starting transfers between devices: 19.6 us -> 30.4 us
    all_gather x1 -> x0, waiting for transfers between devices: 31.6 us -> none  [shards(): gathered = lax.all_gather(features, 'rep', axis=1, tiled=True)]
    reduce_scatter x1, waiting for transfers between devices: 30.4 us -> 0.01 us  [shards(): lax.psum_scatter(partial_terms, 'rep', scatter_dimension=1, tiled=True)]
    ppermute x0 -> x3, waiting for transfers between devices: none -> 14 us  [shards(): lax.ppermute(ring[-1], 'rep', [(dev, (dev + 1) % 4) for dev in range(4)])]
  transfers between devices with their start and end apart: 5 -> 7, of which waited for: 5 -> 6; matrix products, arithmetic and copies ran while one was open for 1% -> 1% of each run, Pallas kernels for 0% -> 0%
where the time goes in v1:
time: 693 us; the launch traced here: 691 us
  waiting for transfers between devices  337 us (49%)
  blocking collectives  128 us (18%)
  other arithmetic  92.6 us (13%)
  local copies, waits for them, and re-layouts  62.4 us (9%)
  starting transfers between devices  30.4 us (4%)
  matrix products  25 us (4%)
  between operations  15.7 us (2%)
    all_to_all x1, waiting for transfers between devices, shards(): lax.all_to_all(outbound, 'dom', split_axis=0, concat_axis=0, tiled=True)  182 us
    psum x1, blocking collectives, shards(): grad_weight, grad_bias = lax.psum((weight_part, bias_part), 'dom')  128 us
    all_to_all x1, waiting for transfers between devices, receive_blocks(): lax.all_to_all(outgoing, 'dom', split_axis=0, concat_axis=0, tiled=True)  94.3 us
    psum x1, waiting for transfers between devices, shards(): grad_weight, grad_bias = lax.psum((weight_part, bias_part), 'dom')  47.5 us
    scatter-add x1, other arithmetic, shards(): per_slot = jax.ops.segment_sum(contrib, tile_sources, NB + peer_count * CAP)  33.2 us
    scatter-add x1, other arithmetic, shards(): aggregate = jax.ops.segment_sum(product, tile_rows, NB + 1)[:NB]  21.1 us
    all_to_all x1, starting transfers between devices, receive_blocks(): lax.all_to_all(outgoing, 'dom', split_axis=0, concat_axis=0, tiled=True)  18 us
    scatter-add x1, other arithmetic, shards(): jax.ops.segment_sum(returned.reshape(peer_count * CAP, B, panel_width), t...  17 us
  transfers between devices with their start and end apart: 7, of which 6 were waited for; matrix products, arithmetic and copies ran while one was open for 1% of the time, Pallas kernels for 0%

profile of v1, /device:TPU:1, one launch (start us, length us, event | category | flops | bytes accessed | tf_op | source)
XLA Modules:
  0.0 691.3 jit_solution(8917627142043339561)
XLA Ops:
  8.0 2.1 collective-permute-start
  10.1 5.2 collective-permute-done
  15.4 1.9 collective-permute-start.1
  18.8 3.7 collective-permute-done.1
  23.9 5.0 collective-permute-done.2
  30.6 1.0 constant_dynamic-update-slice_fusion
  32.1 3.0 gather_fusion
  35.1 4.5 broadcast_select_fusion.1
  39.6 18.0 %all-to-all-start = ((bf16[64,2,128,128]{3,2,1,0:T(8,128)(2,1)}), bf16[64,2,128,128]{3,2,1,0:T(8,128)(2,1)}, u32[]{:S(2)}, u32[]{:S(2)}) async-start(bf16[64,2,128,128]{3,2,1,0:T(8,128)(2,1)} %broadcast_select_fusion.1), calls=%async_computation | async-start | bytes 8388608 | tf_op jit(solution)/shard_map/all_to_all | solution.py:12
  57.7 94.3 %all-to-all-done = bf16[64,2,128,128]{3,2,1,0:T(8,128)(2,1)} async-done(((bf16[64,2,128,128]{3,2,1,0:T(8,128)(2,1)}), bf16[64,2,128,128]{3,2,1,0:T(8,128)(2,1)}, u32[]{:S(2)}, u32[]{:S(2)}) %all-to-all-start) | async-done | bytes 4194336 | tf_op jit(solution)/shard_map/all_to_all | solution.py:12
  152.0 4.6 pad_maximum_fusion
  156.7 10.0 %gather_fusion.1 = bf16[160,128,128]{2,1,0:T(8,128)(2,1)} fusion(bf16[136,128,128]{2,1,0:T(8,128)(2,1)} %pad_maximum_fusion, s32[1024]{0:T(1024)S(1)} %pad_clamp_fusion.1), kind=kCustom, calls=%fused_computation.1 | custom fusion | bytes 10486400 | tf_op jit(solution)/shard_map/gather | solution.py:40
  166.7 11.8 %fusion.4 = f32[160,128,128]{1,2,0:T(8,128)} fusion(bf16[160,128,128]{2,1,0:T(8,128)(2,1)} %gather_fusion.1, bf16[1,160,128,128]{3,2,1,0:T(8,128)(2,1)} %param.13), kind=kOutput, calls=%fused_computation.13 | convolution fusion | flops 671088640 | bytes 20971520 | tf_op jit(solution)/shard_map/kab,kbf->kaf/dot_general | solution.py:39
  178.5 11.7 %copy.19 = f32[160,128,128]{2,1,0:T(8,128)} copy(f32[160,128,128]{1,2,0:T(8,128)} %fusion.4) | data formatting | bytes 20971520 | tf_op jit(solution)/shard_map/kab,kbf->kaf/dot_general | solution.py:39
  190.3 21.1 %scatter_fusion = f32[9,128,128]{2,1,0:T(8,128)S(1)} fusion(f32[9,128,128]{2,1,0:T(8,128)S(1)} %broadcast_in_dim.19, s32[160]{0:T(256)S(1)} %bitcast.54, f32[160,128,128]{2,1,0:T(8,128)} %copy.19), kind=kCustom, calls=%fused_computation.3 | custom fusion | flops 2621440 | bytes 31457920 | tf_op jit(solution)/shard_map/scatter-add | solution.py:42
  212.5 7.5 %gather_fusion.2 = bf16[160,128,128]{2,1,0:T(8,128)(2,1)} fusion(bf16[9,128,128]{2,1,0:T(8,128)(2,1)S(1)} %concatenate.14, s32[1024]{0:T(1024)S(1)} %get-tuple-element.7), kind=kCustom, calls=%fused_computation.2 | custom fusion | bytes 10486400 | tf_op jit(solution)/shard_map/gather | solution.py:53
  220.0 9.8 %fusion.7 = f32[160,128,128]{1,2,0:T(8,128)} fusion(bf16[160,128,128]{2,1,0:T(8,128)(2,1)} %gather_fusion.2, bf16[1,160,128,128]{3,2,1,0:T(8,128)(2,1)} %param.13), kind=kOutput, calls=%fused_computation.14 | convolution fusion | flops 671088640 | bytes 20971520 | tf_op jit(solution)/shard_map/kab,kaf->kbf/dot_general | solution.py:52
  229.8 11.8 %copy.21 = f32[160,128,128]{2,1,0:T(8,128)} copy(f32[160,128,128]{1,2,0:T(8,128)} %fusion.7) | data formatting | bytes 20971520 | tf_op jit(solution)/shard_map/kab,kaf->kbf/dot_general | solution.py:52
  241.6 4.6 broadcast_in_dim.38
  246.1 33.2 %scatter_fusion.1 = f32[136,128,128]{2,1,0:T(8,128)} fusion(f32[136,128,128]{2,1,0:T(8,128)} %broadcast_in_dim.38, s32[160]{0:T(256)S(1)} %bitcast.55, f32[160,128,128]{2,1,0:T(8,128)} %copy.21), kind=kCustom, calls=%fused_computation.4 | custom fusion | flops 2621440 | bytes 31457920 | tf_op jit(solution)/shard_map/scatter-add | solution.py:55
  279.3 7.9 %slice.20 = f32[128,128,128]{2,1,0:T(8,128)} slice(f32[136,128,128]{2,1,0:T(8,128)} %scatter_fusion.1), slice={[8:136], [0:128], [0:128]} | slice | bytes 16777216 | tf_op jit(solution)/shard_map/slice | solution.py:56
  287.2 7.6 %all-to-all-start.1 = ((f32[64,2,128,128]{3,2,1,0:T(8,128)}), f32[64,2,128,128]{3,2,1,0:T(8,128)}, u32[]{:S(2)}, u32[]{:S(2)}) async-start(f32[64,2,128,128]{3,2,1,0:T(8,128)} %bitcast.48), calls=%async_computation.1 | async-start | bytes 16777216 | tf_op jit(solution)/shard_map/all_to_all | solution.py:57
  295.1 1.1 slice.19
  296.2 181.5 %all-to-all-done.1 = f32[64,2,128,128]{3,2,1,0:T(8,128)} async-done(((f32[64,2,128,128]{3,2,1,0:T(8,128)}), f32[64,2,128,128]{3,2,1,0:T(8,128)}, u32[]{:S(2)}, u32[]{:S(2)}) %all-to-all-start.1) | async-done | bytes 8388640 | tf_op jit(solution)/shard_map/all_to_all | solution.py:57
  477.7 7.2 %broadcast_select_fusion = f32[64,2,128,128]{3,2,1,0:T(8,128)} fusion(f32[64,2,128,128]{3,2,1,0:T(8,128)} %all-to-all-done.1, pred[64,2]{1,0:T(8,128)(4,1)S(1)} %iota_compare_fusion), kind=kLoop, calls=%fused_computation.11 | loop fusion | flops 2097152 | bytes 16777344 | tf_op jit(solution)/shard_map/jit(_where)/select_n | solution.py:59
  484.9 17.0 %scatter_fusion.2 = f32[8,128,128]{2,1,0:T(8,128)S(1)} fusion(f32[8,128,128]{2,1,0:T(8,128)S(1)} %slice.19, s32[128]{0:T(128)S(1)} %reshape.185, f32[128,128,128]{2,1,0:T(8,128)} %bitcast.49), kind=kCustom, calls=%fused_computation.5 | custom fusion | flops 2097152 | bytes 25166336 | tf_op jit(solution)/shard_map/scatter-add | solution.py:60
  502.0 1.8 fusion.15
  503.9 1.2 fusion.10
  505.1 127.8 %psum.15 = f32[128]{0:T(128)} all-reduce(f32[128]{0:T(128)S(1)} %get-tuple-element.4), channel_id=1, replica_groups=mesh['dom'=64,'rep'=4] {'dom'}, use_global_device_ids=true, to_apply=%region_6.7 | all-reduce | flops 128 | bytes 1024 | tf_op jit(solution)/shard_map/psum | solution.py:66
  632.9 1.8 convert_element_type.34
  634.6 47.5 %all-reduce.3.cloned.1.call-done = f32[512,128]{1,0:T(8,128)} async-done(((f32[512,128]{1,0:T(8,128)}), f32[512,128]{1,0:T(8,128)}) %all-reduce.3.cloned.1.call-update) | async-done | bytes 262160 | tf_op jit(solution)/shard_map/psum | solution.py:66
  682.1 1.7 copy.36
  (42 shorter events, 6.5 us)
Async XLA Ops:
  8.0 23.6 %copy-start = (bf16[512,128]{1,0:T(8,128)(2,1)S(1)}, bf16[512,128]{1,0:T(8,128)(2,1)}, u32[]{:S(2)}) copy-start(bf16[512,128]{1,0:T(8,128)(2,1)} %param.10) | copy-start | bytes 393220
  8.0 7.4 %collective-permute-start = (bf16[1024,128]{1,0:T(8,128)(2,1)}, bf16[1024,128]{1,0:T(8,128)(2,1)S(1)}, u32[]{:S(2)}, u32[]{:S(2)}) collective-permute-start(bf16[1024,128]{1,0:T(8,128)(2,1)} %param.9), channel_id=1, source_target_pairs={{0,1},{1,2},{2,3},{3,0},{4,5},{5,6},{6,7},{7,4},{8,9},{9,10},{10,1... | collective-permute-start | bytes 786440 | tf_op jit(solution)/shard_map/ppermute | solution.py:23
  15.4 7.2 %collective-permute-start.1 = (bf16[1024,128]{1,0:T(8,128)(2,1)S(1)}, bf16[1024,128]{1,0:T(8,128)(2,1)S(1)}, u32[]{:S(2)}, u32[]{:S(2)}) collective-permute-start(bf16[1024,128]{1,0:T(8,128)(2,1)S(1)} %collective-permute-done), channel_id=1, source_target_pairs={{0,1},{1,2},{2,3},{3,0},{4,5},{5,6},{6,7},{7,4},{8,9},{9,10},{10,1... | collective-permute-start | bytes 786440 | tf_op jit(solution)/shard_map/ppermute | solution.py:23
  22.5 6.4 collective-permute-start.2
  39.6 18.1 %copy-start.5 = (bf16[128]{0:T(256)(128)(2,1)S(1)}, bf16[128]{0:T(256)(128)(2,1)}, u32[]{:S(2)}) copy-start(bf16[128]{0:T(256)(128)(2,1)} %param.11) | copy-start | bytes 772
  39.6 18.1 %copy-start.3 = (s32[1,160]{1,0:T(1,128)S(1)}, s32[1,160]{1,0:T(1,128)}, u32[]{:S(2)}) copy-start(s32[1,160]{1,0:T(1,128)} %param.15) | copy-start | bytes 1924
  39.6 112.4 %all-to-all-start = ((bf16[64,2,128,128]{3,2,1,0:T(8,128)(2,1)}), bf16[64,2,128,128]{3,2,1,0:T(8,128)(2,1)}, u32[]{:S(2)}, u32[]{:S(2)}) async-start(bf16[64,2,128,128]{3,2,1,0:T(8,128)(2,1)} %broadcast_select_fusion.1), calls=%async_computation | async-start | bytes 8388608 | tf_op jit(solution)/shard_map/all_to_all | solution.py:12
  178.5 11.8 %copy-start.2 = (s32[1,160]{1,0:T(1,128)S(1)}, s32[1,160]{1,0:T(1,128)}, u32[]{:S(2)}) copy-start(s32[1,160]{1,0:T(1,128)} %param.14) | copy-start | bytes 1924
  190.3 21.2 %copy-start.1 = (bf16[1024,128]{1,0:T(8,128)(2,1)S(1)}, bf16[1024,128]{1,0:T(8,128)(2,1)}, u32[]{:S(2)}) copy-start(bf16[1024,128]{1,0:T(8,128)(2,1)} %param.12) | copy-start | bytes 786436
  287.2 7.7 %copy-start.4 = (s32[1,64,2]{1,2,0:T(2,128)S(1)}, s32[1,64,2]{1,2,0:T(2,128)}, u32[]{:S(2)}) copy-start(s32[1,64,2]{1,2,0:T(2,128)} %param.16) | copy-start | bytes 1540
  287.2 190.5 %all-to-all-start.1 = ((f32[64,2,128,128]{3,2,1,0:T(8,128)}), f32[64,2,128,128]{3,2,1,0:T(8,128)}, u32[]{:S(2)}, u32[]{:S(2)}) async-start(f32[64,2,128,128]{3,2,1,0:T(8,128)} %bitcast.48), calls=%async_computation.1 | async-start | bytes 16777216 | tf_op jit(solution)/shard_map/all_to_all | solution.py:57
  294.8 338.0 %reduce-scatter.2.cloned.1.call-start = ((), (), s32[]{:S(2)}) async-start(), calls=%async_computation.3 | async-start | bytes 2621440 | tf_op jit(solution)/shard_map/reduce_scatter | solution.py:68
  503.8 178.3 %all-reduce.3.cloned.1.call-start = ((), (), s32[]{:S(2)}) async-start(), calls=%async_computation.4 | async-start | bytes 524288 | tf_op jit(solution)/shard_map/psum | solution.py:66
Sparse Core Ops, SparseCore 0:
  503.9 30.1 reduce-scatter.1
Sparse Core Ops, SparseCore 1:
  508.8 173.3 all-reduce.2
